TPU v7x, 128 devices: a whole 4x4x4 slice. The times are simulated.
128 devices in a mesh: row: 16 (over x, y), col: 8 (over z, core).
Axes of the slice: x: 4, y: 4, z: 4, core: 2. Of those that a mesh axis runs over, the one named last changes fastest.
Arguments:
- amp_store: bfloat16 [32768, 1024], P(('row', 'col')), may hold values from -6 to 6
- store_map: int32 [32768], P(('row', 'col')), may hold values from 0 to 32767, as said below
- integrals: bfloat16 [32768, 32768], P('row', 'col'), may hold values from -0.09375 to 0.09375
- occ_irrep: int32 [100], replicated, may hold values from 0 to 7
- virt_irrep: int32 [800], replicated, may hold values from 0 to 7
- occ_orbs: int32 [2, 1024], replicated, may hold values from 0 to 99
- k_orbs: int32 [2, 32768], P(None, 'col'), may hold values from 0 to 799
- m_orbs: int32 [2, 32768], P(None, 'row'), may hold values from 0 to 799
Outputs:
- ladder: bfloat16 [32768, 1024], P('row', 'col')
Inputs may be any that keep to these rules, and one draw needn't show every extreme that they name: store_map is a permutation. Grid position k belongs to the block of device (r, c) with c = k // 4096 and r = (k % 4096) // 256; the stored rows of device s = r' * 8 + c' (its shard of amp_store) send exactly 2 rows to every device's block, and within block (r, c) those rows fill positions s * 2 to s * 2 + 1.
All inputs are finite; a program needn't handle non-finite values.
Results may differ from a plain program's by a relative error of at most 0.001.
Values may be sent and summed in bfloat16 or wider, within the bound.
No kernel may reach another device: no remote copies, remote signals or barrier semaphores. Data moves between devices by JAX's collectives and lax.ppermute only.
A program may use at most 192 MiB of HBM per device.

v0:
```python
import jax
import jax.numpy as jnp
from jax import lax
from jax.sharding import PartitionSpec as P


def pair_irrep(labels, orbitals):
    return jnp.bitwise_xor(labels[orbitals[0]], labels[orbitals[1]])


def redistribute(buffer):
    return lax.all_to_all(buffer, ("row", "col"), split_axis=0, concat_axis=0, tiled=True)


def body(amp_store, store_map, integrals, occ_irrep, virt_irrep, occ_orbs, k_orbs, m_orbs):
    row_count = lax.axis_size("row")
    col_count = lax.axis_size("col")
    dev_count = row_count * col_count
    stored = amp_store.shape[0]
    slot_count = stored // dev_count
    kblock = k_orbs.shape[1]
    my_row = lax.axis_index("row")
    my_col = lax.axis_index("col")
    myself = my_row * col_count + my_col
    occ_sym = pair_irrep(occ_irrep, occ_orbs)
    k_sym = pair_irrep(virt_irrep, k_orbs)
    m_sym = pair_irrep(virt_irrep, m_orbs)
    naught = jnp.zeros((), amp_store.dtype)
    owner_col = store_map // kblock
    owner_row = store_map % kblock // stored
    within = store_map % stored - myself * slot_count
    place = (owner_row * col_count + owner_col) * slot_count + within
    ordered = jnp.zeros_like(amp_store).at[place].set(amp_store)
    grid_rows = redistribute(ordered)
    own_sym = lax.dynamic_slice_in_dim(k_sym, my_row * stored, stored)
    masked = jnp.where(own_sym[:, None] == occ_sym[None, :], grid_rows, naught)
    screened = jnp.where(m_sym[:, None] == k_sym[None, :], integrals, naught)
    partial_sum = jnp.dot(
        screened,
        lax.all_gather(masked, "row", axis=0, tiled=True),
        preferred_element_type=jnp.float32,
    )
    return lax.psum_scatter(partial_sum, "col", scatter_dimension=1, tiled=True).astype(
        jnp.bfloat16
    )


def solution(mesh):
    in_specs = (
        P(("row", "col"), None),
        P(("row", "col")),
        P("row", "col"),
        P(),
        P(),
        P(),
        P(None, "col"),
        P(None, "row"),
    )
    out_specs = P("row", "col")
    return jax.shard_map(body, mesh=mesh, in_specs=in_specs, out_specs=out_specs, check_vma=False)
```

profile of v0, /device:TPU:1, one launch (start us, length us, event | category | flops | bytes accessed | tf_op | source)
XLA Modules:
  0.0 227.8 jit_solution(790989512550864099)
XLA Ops:
  6.5 0.0 copy-start
  6.5 0.7 compare_select_fusion.9
  7.3 2.3 %scatter_custom_fusion = bf16[256,1024]{1,0:T(8,128)(2,1)S(1)} fusion(s32[256]{0:T(256)S(1)} %compare_select_fusion.9, bf16[256,1024]{1,0:T(8,128)(2,1)} %param.8, bf16[]{:T(256)} %constant.62.clone.1), kind=kCustom, calls=%fused_computation.13 | custom fusion | bytes 524800 | tf_op jit(solution)/shard_map/scatter | solution.py:33
  9.6 1.0 all_to_all.8
  10.6 11.5 %all-to-all-start = ((bf16[128,2,1024]{2,1,0:T(2,128)(2,1)}), bf16[128,2,1024]{2,1,0:T(2,128)(2,1)S(1)}, u32[]{:S(2)}, u32[]{:S(2)}) async-start(bf16[128,2,1024]{2,1,0:T(2,128)(2,1)} %all_to_all.8), calls=%async_computation | async-start | bytes 1048576 | tf_op jit(solution)/shard_map/all_to_all | solution.py:12
  22.1 0.0 all-gather.2.cloned.1.call-start
  22.1 0.8 compare_select_fusion.7
  22.9 0.9 compare_select_fusion.3
  23.8 5.9 %gather_fusion.5 = s32[1024]{0:T(1024)S(1)} fusion(s32[100]{0:T(128)} %param.11, s32[1024]{0:T(1024)S(1)} %broadcast_clamp_fusion.4), kind=kCustom, calls=%fused_computation.5 | custom fusion | bytes 12288 | tf_op jit(solution)/shard_map/gather | solution.py:8
  29.7 5.9 %gather_fusion.4 = s32[1024]{0:T(1024)S(1)} fusion(s32[100]{0:T(128)} %param.11, s32[1024]{0:T(1024)S(1)} %broadcast_clamp_fusion.5), kind=kCustom, calls=%fused_computation.4 | custom fusion | bytes 12288 | tf_op jit(solution)/shard_map/gather | solution.py:8
  35.5 0.0 copy-done
  35.5 0.0 copy-start.1
  35.6 16.7 %gather_fusion.3 = s32[4096]{0:T(1024)S(1)} fusion(s32[800]{0:T(1024)S(1)} %copy-done, s32[4096]{0:T(1024)S(1)} %broadcast_clamp_fusion), kind=kCustom, calls=%fused_computation.3 | custom fusion | bytes 49152 | tf_op jit(solution)/shard_map/gather | solution.py:8
  52.3 16.7 %gather_fusion.2 = s32[4096]{0:T(1024)S(1)} fusion(s32[800]{0:T(1024)S(1)} %copy-done, s32[4096]{0:T(1024)S(1)} %broadcast_clamp_fusion.1), kind=kCustom, calls=%fused_computation.2 | custom fusion | bytes 49152 | tf_op jit(solution)/shard_map/gather | solution.py:8
  69.0 0.1 dynamic_slice.3
  69.1 0.0 all-to-all-done
  69.1 0.2 all_to_all.10
  69.3 1.0 compare_select_fusion.2
  70.3 0.0 all-gather.2.cloned.1.call-update
  70.3 0.0 reduce-scatter.2.cloned.1.call-start
  70.3 0.0 copy-done.1
  70.4 8.6 %gather_fusion.1 = s32[2048]{0:T(1024)S(1)} fusion(s32[800]{0:T(1024)S(1)} %copy-done, s32[2048]{0:T(1024)S(1)} %broadcast_clamp_fusion.2), kind=kCustom, calls=%fused_computation.1 | custom fusion | bytes 24576 | tf_op jit(solution)/shard_map/gather | solution.py:8
  79.0 8.6 %gather_fusion = s32[2048]{0:T(1024)S(1)} fusion(s32[800]{0:T(1024)S(1)} %copy-done, s32[2048]{0:T(1024)S(1)} %broadcast_clamp_fusion.3), kind=kCustom, calls=%fused_computation | custom fusion | bytes 24576 | tf_op jit(solution)/shard_map/gather | solution.py:8
  87.6 54.9 %all-gather.2.cloned.1.call-done = bf16[4096,1024]{1,0:T(8,128)(2,1)} async-done(((bf16[256,1024]{1,0:T(8,128)(2,1)}), bf16[4096,1024]{1,0:T(8,128)(2,1)}) %all-gather.2.cloned.1.call-update) | async-done | bytes 8388624 | tf_op jit(solution)/shard_map/all_gather | solution.py:40
  142.5 24.6 %fusion = f32[2048,1024]{1,0:T(8,128)} fusion(bf16[4096,1024]{1,0:T(8,128)(2,1)} %all-gather.2.cloned.1.call-done, bf16[2048,4096]{1,0:T(8,128)(2,1)} %param.10, s32[4096]{0:T(1024)S(1)} %xor.22, s32[2048]{0:T(1024)S(1)} %xor.21), kind=kOutput, calls=%fused_computation.8 | convolution fusion | flops 17196646400 | bytes 33579008 | tf_op jit(solution)/shard_map/dot_general | solution.py:38
  167.1 0.0 reduce-scatter.2.cloned.1.call-update
  167.1 51.8 %reduce-scatter.2.cloned.1.call-done = f32[2048,128]{1,0:T(8,128)} async-done(((f32[2048,1024]{1,0:T(8,128)}), f32[2048,128]{1,0:T(8,128)}) %reduce-scatter.2.cloned.1.call-update) | async-done | bytes 1048592 | tf_op jit(solution)/shard_map/reduce_scatter | solution.py:43
  218.9 2.1 convert_element_type.3
  (10 shorter events, 0.1 us)
Async XLA Ops:
  6.5 29.0 %copy-start = (s32[800]{0:T(1024)S(1)}, s32[800]{0:T(1024)}, u32[]{:S(2)}) copy-start(s32[800]{0:T(1024)} %param.12) | copy-start | bytes 9604
  10.6 58.5 %all-to-all-start = ((bf16[128,2,1024]{2,1,0:T(2,128)(2,1)}), bf16[128,2,1024]{2,1,0:T(2,128)(2,1)S(1)}, u32[]{:S(2)}, u32[]{:S(2)}) async-start(bf16[128,2,1024]{2,1,0:T(2,128)(2,1)} %all_to_all.8), calls=%async_computation | async-start | bytes 1048576 | tf_op jit(solution)/shard_map/all_to_all | solution.py:12
  22.1 120.5 %all-gather.2.cloned.1.call-start = ((), (), s32[]{:S(2)}) async-start(), calls=%async_computation.2 | async-start | bytes 8912896 | tf_op jit(solution)/shard_map/all_gather | solution.py:40
  35.5 34.8 %copy-start.1 = (s32[2,2048]{1,0:T(2,128)S(1)}, s32[2,2048]{1,0:T(2,128)}, u32[]{:S(2)}) copy-start(s32[2,2048]{1,0:T(2,128)} %param.15) | copy-start | bytes 49156
  70.3 148.7 %reduce-scatter.2.cloned.1.call-start = ((), (), s32[]{:S(2)}) async-start(), calls=%async_computation.3 | async-start | bytes 9437184 | tf_op jit(solution)/shard_map/reduce_scatter | solution.py:43
Sparse Core Ops, SparseCore 0:
  70.4 72.0 all-gather.1
  167.2 51.6 reduce-scatter.1
where the time goes:
time: 228 us
  waiting for transfers between devices  107 us (47%)
  local copies, waits for them, and re-layouts  65.8 us (29%)
  matrix products  24.6 us (11%)
  between operations  13.6 us (6%)
  starting transfers between devices  11.6 us (5%)
  other arithmetic  5.5 us (2%)
    gather x6, local copies, waits for them, and re-layouts, pair_irrep(): return jnp.bitwise_xor(labels[orbitals[0]], labels[orbitals[1]])  62.2 us
    all_gather x1, waiting for transfers between devices, body(): lax.all_gather(masked, 'row', axis=0, tiled=True)  54.9 us
    reduce_scatter x1, waiting for transfers between devices, body(): lax.psum_scatter(partial_sum, 'col', scatter_dimension=1, tiled=True)  51.8 us
    dot_general x1, matrix products, body(): jnp.dot(screened, lax.all_gather(masked, 'row', axis=0, tiled=True), pref...  24.6 us
    all_to_all x1, starting transfers between devices, redistribute(): lax.all_to_all(buffer, ('row', 'col'), split_axis=0, concat_axis=0, tiled...  11.5 us
  transfers between devices with their start and end apart: 3, of which 2 were waited for; matrix products, arithmetic and copies ran while one was open for 28% of the time, Pallas kernels for 0%

commit v1 on v0

--- a/solution.py
+++ b/solution.py
@@ -37,7 +37,9 @@
     screened = jnp.where(m_sym[:, None] == k_sym[None, :], integrals, naught)
     partial_sum = jnp.dot(
         screened,
-        lax.all_gather(masked, "row", axis=0, tiled=True),
+        jnp.concatenate(
+            lax.all_to_all(jnp.stack([masked] * lax.axis_size("row")), "row", 0, 0), axis=0
+        ),
         preferred_element_type=jnp.float32,
     )
     return lax.psum_scatter(partial_sum, "col", scatter_dimension=1, tiled=True).astype(

time: 228 us -> 322 us (1.41)
  waiting for transfers between devices: 107 us -> 188 us
  starting transfers between devices: 11.6 us -> 18.3 us
  local copies, waits for them, and re-layouts: 65.8 us -> 71.6 us
    all_to_all x0 -> x1, waiting for transfers between devices: none -> 127 us  [body(): lax.all_to_all(jnp.stack([masked] * lax.axis_size('row')), 'row', 0, 0)]
    all_gather x1 -> x0, waiting for transfers between devices: 54.9 us -> none  [body(): lax.all_gather(masked, 'row', axis=0, tiled=True)]
    reduce_scatter x1, waiting for transfers between devices: 51.8 us -> 61 us  [body(): lax.psum_scatter(partial_sum, 'col', scatter_dimension=1, tiled=True)]
    all_to_all x0 -> x1, starting transfers between devices: none -> 6.74 us  [body(): lax.all_to_all(jnp.stack([masked] * lax.axis_size('row')), 'row', 0, 0)]
    another operation x0 -> x1, local copies, waits for them, and re-layouts: none -> 4.34 us  [body(): jnp.stack([masked] * lax.axis_size('row'))]
  transfers between devices with their start and end apart: 3 -> 3, of which waited for: 2 -> 2; matrix products, arithmetic and copies ran while one was open for 28% -> 20% of each run, Pallas kernels for 0% -> 0%
where the time goes in v1:
time: 322 us; the launch traced here: 321 us
  waiting for transfers between devices  188 us (58%)
  local copies, waits for them, and re-layouts  71.6 us (22%)
  matrix products  24.5 us (8%)
  starting transfers between devices  18.3 us (6%)
  between operations  13.6 us (4%)
  other arithmetic  4.7 us (1%)
    all_to_all x1, waiting for transfers between devices, body(): lax.all_to_all(jnp.stack([masked] * lax.axis_size('row')), 'row', 0, 0)  127 us
    gather x6, local copies, waits for them, and re-layouts, pair_irrep(): return jnp.bitwise_xor(labels[orbitals[0]], labels[orbitals[1]])  63.7 us
    reduce_scatter x1, waiting for transfers between devices, body(): lax.psum_scatter(partial_sum, 'col', scatter_dimension=1, tiled=True)  61 us
    dot_general x1, matrix products, body(): jnp.dot(screened, jnp.concatenate(lax.all_to_all(jnp.stack([masked] * lax...  24.5 us
    all_to_all x1, starting transfers between devices, redistribute(): lax.all_to_all(buffer, ('row', 'col'), split_axis=0, concat_axis=0, tiled...  11.5 us
    all_to_all x1, starting transfers between devices, body(): lax.all_to_all(jnp.stack([masked] * lax.axis_size('row')), 'row', 0, 0)  6.74 us
  transfers between devices with their start and end apart: 3, of which 2 were waited for; matrix products, arithmetic and copies ran while one was open for 20% of the time, Pallas kernels for 0%

profile of v1, /device:TPU:1, one launch (start us, length us, event | category | flops | bytes accessed | tf_op | source)
XLA Modules:
  0.0 321.2 jit_solution(3259932837545769332)
XLA Ops:
  6.5 0.0 copy-start
  6.5 0.7 compare_select_fusion.9
  7.3 2.3 scatter_custom_fusion
  9.6 1.0 all_to_all.11
  10.6 11.5 %all-to-all-start = ((bf16[128,2,1024]{2,1,0:T(2,128)(2,1)}), bf16[128,2,1024]{2,1,0:T(2,128)(2,1)S(1)}, u32[]{:S(2)}, u32[]{:S(2)}) async-start(bf16[128,2,1024]{2,1,0:T(2,128)(2,1)} %all_to_all.11), calls=%async_computation | async-start | bytes 1048576 | tf_op jit(solution)/shard_map/all_to_all | solution.py:12
  22.1 0.9 compare_select_fusion.3
  23.0 0.8 compare_select_fusion.7
  23.8 0.0 copy-done
  23.8 0.0 copy-start.1
  23.8 16.7 %gather_fusion.2 = s32[4096]{0:T(1024)S(1)} fusion(s32[800]{0:T(1024)S(1)} %copy-done, s32[4096]{0:T(1024)S(1)} %broadcast_clamp_fusion.1), kind=kCustom, calls=%fused_computation.2 | custom fusion | bytes 49152 | tf_op jit(solution)/shard_map/gather | solution.py:8
  40.5 16.7 %gather_fusion.3 = s32[4096]{0:T(1024)S(1)} fusion(s32[800]{0:T(1024)S(1)} %copy-done, s32[4096]{0:T(1024)S(1)} %broadcast_clamp_fusion), kind=kCustom, calls=%fused_computation.3 | custom fusion | bytes 49152 | tf_op jit(solution)/shard_map/gather | solution.py:8
  57.2 0.0 copy-done.1
  57.2 6.6 %gather_fusion.4 = s32[1024]{0:T(1024)S(1)} fusion(s32[100]{0:T(128)S(1)} %copy-done.1, s32[1024]{0:T(1024)S(1)} %broadcast_clamp_fusion.5), kind=kCustom, calls=%fused_computation.4 | custom fusion | bytes 12288 | tf_op jit(solution)/shard_map/gather | solution.py:8
  63.8 0.0 copy-start.2
  63.8 6.6 %gather_fusion.5 = s32[1024]{0:T(1024)S(1)} fusion(s32[100]{0:T(128)S(1)} %copy-done.1, s32[1024]{0:T(1024)S(1)} %broadcast_clamp_fusion.4), kind=kCustom, calls=%fused_computation.5 | custom fusion | bytes 12288 | tf_op jit(solution)/shard_map/gather | solution.py:8
  70.4 0.1 dynamic_slice.3
  70.5 0.0 all-to-all-done
  70.5 0.2 all_to_all.13
  70.7 0.2 compare_select_fusion.2
  70.9 4.3 %stack.2 = bf16[16,256,1024]{2,1,0:T(8,128)(2,1)} broadcast(bf16[256,1024]{1,0:T(8,128)(2,1)S(1)} %compare_select_fusion.2), dimensions={1,2} | broadcast | bytes 8912896 | tf_op jit(solution)/shard_map/stack | solution.py:41
  75.2 6.7 %all-to-all-start.1 = ((bf16[16,256,1024]{2,1,0:T(8,128)(2,1)}), bf16[16,256,1024]{2,1,0:T(8,128)(2,1)}, u32[]{:S(2)}, u32[]{:S(2)}) async-start(bf16[16,256,1024]{2,1,0:T(8,128)(2,1)} %stack.2), calls=%async_computation.1 | async-start | bytes 16777216 | tf_op jit(solution)/shard_map/all_to_all | solution.py:41
  82.0 0.0 reduce-scatter.2.cloned.1.call-start
  82.0 0.0 copy-done.2
  82.1 8.6 %gather_fusion = s32[2048]{0:T(1024)S(1)} fusion(s32[800]{0:T(1024)S(1)} %copy-done, s32[2048]{0:T(1024)S(1)} %broadcast_clamp_fusion.3), kind=kCustom, calls=%fused_computation | custom fusion | bytes 24576 | tf_op jit(solution)/shard_map/gather | solution.py:8
  90.7 8.6 %gather_fusion.1 = s32[2048]{0:T(1024)S(1)} fusion(s32[800]{0:T(1024)S(1)} %copy-done, s32[2048]{0:T(1024)S(1)} %broadcast_clamp_fusion.2), kind=kCustom, calls=%fused_computation.1 | custom fusion | bytes 24576 | tf_op jit(solution)/shard_map/gather | solution.py:8
  99.3 127.5 %all-to-all-done.1 = bf16[16,256,1024]{2,1,0:T(8,128)(2,1)} async-done(((bf16[16,256,1024]{2,1,0:T(8,128)(2,1)}), bf16[16,256,1024]{2,1,0:T(8,128)(2,1)}, u32[]{:S(2)}, u32[]{:S(2)}) %all-to-all-start.1) | async-done | bytes 8388640 | tf_op jit(solution)/shard_map/all_to_all | solution.py:41
  226.8 24.5 %fusion = f32[2048,1024]{1,0:T(8,128)} fusion(bf16[4096,1024]{1,0:T(8,128)(2,1)} %bitcast.12, bf16[2048,4096]{1,0:T(8,128)(2,1)} %param.10, s32[4096]{0:T(1024)S(1)} %xor.22, s32[2048]{0:T(1024)S(1)} %xor.21), kind=kOutput, calls=%fused_computation.8 | convolution fusion | flops 17196646400 | bytes 33579008 | tf_op jit(solution)/shard_map/dot_general | solution.py:38
  251.3 0.0 reduce-scatter.2.cloned.1.call-update
  251.3 61.0 %reduce-scatter.2.cloned.1.call-done = f32[2048,128]{1,0:T(8,128)} async-done(((f32[2048,1024]{1,0:T(8,128)}), f32[2048,128]{1,0:T(8,128)}) %reduce-scatter.2.cloned.1.call-update) | async-done | bytes 1048592 | tf_op jit(solution)/shard_map/reduce_scatter | solution.py:45
  312.3 2.1 convert_element_type.3
  (10 shorter events, 0.1 us)
Async XLA Ops:
  6.5 17.2 %copy-start = (s32[800]{0:T(1024)S(1)}, s32[800]{0:T(1024)}, u32[]{:S(2)}) copy-start(s32[800]{0:T(1024)} %param.12) | copy-start | bytes 9604
  10.6 59.9 %all-to-all-start = ((bf16[128,2,1024]{2,1,0:T(2,128)(2,1)}), bf16[128,2,1024]{2,1,0:T(2,128)(2,1)S(1)}, u32[]{:S(2)}, u32[]{:S(2)}) async-start(bf16[128,2,1024]{2,1,0:T(2,128)(2,1)} %all_to_all.11), calls=%async_computation | async-start | bytes 1048576 | tf_op jit(solution)/shard_map/all_to_all | solution.py:12
  23.8 33.4 %copy-start.1 = (s32[100]{0:T(128)S(1)}, s32[100]{0:T(128)}, u32[]{:S(2)}) copy-start(s32[100]{0:T(128)} %param.11) | copy-start | bytes 1204
  63.8 18.2 %copy-start.2 = (s32[2,2048]{1,0:T(2,128)S(1)}, s32[2,2048]{1,0:T(2,128)}, u32[]{:S(2)}) copy-start(s32[2,2048]{1,0:T(2,128)} %param.15) | copy-start | bytes 49156
  75.2 151.6 %all-to-all-start.1 = ((bf16[16,256,1024]{2,1,0:T(8,128)(2,1)}), bf16[16,256,1024]{2,1,0:T(8,128)(2,1)}, u32[]{:S(2)}, u32[]{:S(2)}) async-start(bf16[16,256,1024]{2,1,0:T(8,128)(2,1)} %stack.2), calls=%async_computation.1 | async-start | bytes 16777216 | tf_op jit(solution)/shard_map/all_to_all | solution.py:41
  82.0 230.3 %reduce-scatter.2.cloned.1.call-start = ((), (), s32[]{:S(2)}) async-start(), calls=%async_computation.3 | async-start | bytes 9437184 | tf_op jit(solution)/shard_map/reduce_scatter | solution.py:45
Sparse Core Ops, SparseCore 0:
  251.4 60.8 reduce-scatter.1
